TPU v7x, 128 devices: a whole 4x4x4 slice. The times are simulated.
128 devices in a mesh: rows: 64 (over z, y, x), seq: 2 (over core).
Axes of the slice: x: 4, y: 4, z: 4, core: 2. Of those that a mesh axis runs over, the one named last changes fastest.
Arguments:
- enc_rows: bfloat16 [32768, 1408], P(('rows', 'seq')), may hold values from -6 to 6
- visible_pos: int32 [32768], P(('rows', 'seq')), may hold values from 0 to 131071, as said below
- enc_norm_gain: float32 [2, 1408], replicated, may hold values from 0.1 to 1.9
- enc_fc1: bfloat16 [1408, 6144], P(None, 'seq'), may hold values from -0.15625 to 0.15625
- enc_fc1_bias: float32 [6144], P('seq'), may hold values from -3 to 3
- enc_fc2: bfloat16 [6144, 1408], P('seq'), may hold values from -0.078125 to 0.078125
- enc_fc2_bias: float32 [1408], replicated, may hold values from -3 to 3
- handoff_weight: bfloat16 [1408, 512], replicated, may hold values from -0.15625 to 0.15625
- mask_token: float32 [512], replicated, may hold values from -4 to 4
- dec_norm_gain: float32 [2, 512], replicated, may hold values from 0.1 to 1.9
- qkv_weight: bfloat16 [512, 1536], replicated
- qkv_bias: float32 [1536], replicated, may hold values from -3 to 3
- out_weight: bfloat16 [512, 512], replicated, may hold values from -0.25 to 0.25
- out_bias: float32 [512], replicated, may hold values from -3 to 3
- dec_fc1: bfloat16 [512, 2048], replicated, may hold values from -0.25 to 0.25
- dec_fc1_bias: float32 [2048], replicated, may hold values from -3 to 3
- dec_fc2: bfloat16 [2048, 512], replicated, may hold values from -0.125 to 0.125
- dec_fc2_bias: float32 [512], replicated, may hold values from -3 to 3
Outputs:
- decoded: bfloat16 [64, 2048, 512], P('rows', 'seq')
Inputs may be any that keep to these rules, and one draw needn't show every extreme that they name: `visible_pos`: all values differ. Number the devices of rows and seq together as d = rows index * 2 + seq index; decoder device d holds clips of rows index and tokens of seq index. Every decoder device's block receives at most 768 visible tokens, and one device's block receives exactly that many in every draw. The visible tokens of all blocks, in order of block and then position, are dealt out one at a time to devices 0, 1, 2, ... in turn, so no device holds more than 6 tokens of one block, and some device holds exactly 6 of one.
All inputs are finite; a program needn't handle non-finite values.
Results may differ from a plain program's by a relative error of at most 0.013.
Values may be sent and summed in bfloat16 or wider, within the bound.
No kernel may reach another device: no remote copies, remote signals or barrier semaphores. Data moves between devices by JAX's collectives and lax.ppermute only.
A program may use at most 256 MiB of HBM per device.

v0:
```python
import math

import jax
import jax.numpy as jnp
import numpy as np
from jax import lax
from jax.experimental import pallas as pl
from jax.experimental.pallas import tpu as pltpu
from jax.sharding import PartitionSpec as P

HEADS = 8
CLIP_LEN = 2048
SPAN = 1024
WIDTH = 512
HEAD_D = 64
GROUP = 16
LABEL_ROW = 12
EPS = 1e-06
F32 = jnp.float32
BF16 = jnp.bfloat16
MIB = 1 << 20
WHOLE = pl.BlockSpec(memory_space=pltpu.VMEM)
SAFE = 60.0
SAFE_VALUE = 2.0**40

def norm(values, gain):
    mean = jnp.mean(values, axis=-1, keepdims=True)
    centered = values - mean
    spread = jnp.mean(centered * centered, axis=-1, keepdims=True)
    return centered * lax.rsqrt(spread + EPS) * gain


def gelu(x):
    half = 0.5 * x
    return half + half * lax.erf(x * (0.5**0.5))


def dot(a, b):
    return jnp.dot(a, b, preferred_element_type=F32)


def iota(shape, dim):
    return lax.broadcasted_iota(jnp.int32, shape, dim)


def sinusoid_parts():
    column = np.arange(WIDTH)
    rate = 10000.0 ** (-(2 * (column // 2)) / WIDTH)
    phase = np.where(column % 2 == 0, 0.0, np.pi / 2)
    coarse = 32.0 * np.arange(CLIP_LEN // 32)[:, None] * rate[None, :] + phase[None, :]
    fine = np.arange(32)[:, None] * rate[None, :]
    return tuple(
        np.asarray(part, np.float32)
        for part in (np.sin(coarse), np.cos(coarse), np.sin(fine), np.cos(fine))
    )


ENC_TILE = 512
IN_FLIGHT = 2
IN_SIZES = (1024, 2048)
OUT_SIZES = (1408,)


def tiles_of(sizes):
    starts = [sum(sizes[:i]) for i in range(len(sizes))]
    return [(start, start + size) for start, size in zip(starts, sizes)]


def cut(start, stop):
    return [pl.ds(at, min(ENC_TILE, stop - at)) for at in range(start, stop, ENC_TILE)]


def enc_kernel(rows_ref, gain_ref, w1_ref, b1_ref, w2_ref, out_ref, w1, w2, rows, gain, b1, hidden,
               arrived, arrived1, arrived2):
    small = [
        pltpu.make_async_copy(source, target, arrived.at[i])
        for i, (source, target) in enumerate(((rows_ref, rows), (gain_ref, gain), (b1_ref, b1)))
    ]
    loads = []
    for sizes, source, target, sems in ((IN_SIZES, w1_ref, w1, arrived1), (OUT_SIZES, w2_ref, w2, arrived2)):
        for i, (start, stop) in enumerate(tiles_of(sizes)):
            tile = pl.ds(start, stop - start)
            loads.append(pltpu.make_async_copy(source.at[:, tile], target.at[:, tile], sems.at[i]))
    for load in small + loads[:IN_FLIGHT]:
        load.start()

    def take(i):
        loads[i].wait()
        if i + IN_FLIGHT < len(loads):
            loads[i + IN_FLIGHT].start()

    for load in small:
        load.wait()
    normed = norm(rows[...].astype(F32), gain[0:1, :]).astype(BF16)
    for i, (start, stop) in enumerate(tiles_of(IN_SIZES)):
        take(i)
        for tile in cut(start, stop):
            hidden[:, tile] = gelu(dot(normed, w1[:, tile]) + b1[:, tile]).astype(BF16)
    for i, (start, stop) in enumerate(tiles_of(OUT_SIZES)):
        take(len(IN_SIZES) + i)
        for tile in cut(start, stop):
            out_ref[:, tile] = dot(hidden[...], w2[:, tile]).astype(BF16)


def enc_cost(count, width, units):
    return pl.CostEstimate(
        flops=4 * count * width * units,
        bytes_accessed=4 * width * units + 4 * count * width,
        transcendentals=count * units,
    )


def first_encoder_mlp(rows, gain, w1, b1, w2):
    count, width = rows.shape
    units = w1.shape[1]
    far = pl.BlockSpec(memory_space=pl.ANY)
    return pl.pallas_call(
        enc_kernel,
        in_specs=[far] * 5,
        out_specs=[WHOLE] * 3,
        out_shape=[
            jax.ShapeDtypeStruct((count, width), BF16),
            jax.ShapeDtypeStruct(w1.shape, BF16),
            jax.ShapeDtypeStruct(w2.shape, BF16),
        ],
        scratch_shapes=[
            pltpu.VMEM((count, width), BF16),
            pltpu.VMEM(gain.shape, F32),
            pltpu.VMEM(b1.shape, F32),
            pltpu.VMEM((count, units), BF16),
            pltpu.SemaphoreType.DMA((3,)),
            pltpu.SemaphoreType.DMA((len(IN_SIZES),)),
            pltpu.SemaphoreType.DMA((len(OUT_SIZES),)),
        ],
        compiler_params=pltpu.CompilerParams(vmem_limit_bytes=FIRST_VMEM),
        cost_estimate=enc_cost(count, width, units),
        name="first_encoder_mlp",
    )(rows, gain, w1, b1, w2)


def second_enc_kernel(rows_ref, gain_ref, w1, b1, w2, out_ref, hidden):
    units, width = w2.shape
    normed = norm(rows_ref[...].astype(F32), gain_ref[0:1, :]).astype(BF16)
    for tile in cut(0, units):
        hidden[:, tile] = gelu(dot(normed, w1[:, tile]) + b1[:, tile]).astype(BF16)
    for tile in cut(0, width):
        out_ref[:, tile] = dot(hidden[...], w2[:, tile]).astype(BF16)


def second_encoder_mlp(rows, gain, w1, b1, w2):
    count, width = rows.shape
    units = w1.shape[1]
    return pl.pallas_call(
        second_enc_kernel,
        in_specs=[WHOLE] * 5,
        out_specs=WHOLE,
        out_shape=jax.ShapeDtypeStruct((count, width), BF16),
        scratch_shapes=[pltpu.VMEM((count, units), BF16)],
        compiler_params=pltpu.CompilerParams(vmem_limit_bytes=ENC_VMEM * MIB),
        cost_estimate=enc_cost(count, width, units),
        name="second_encoder_mlp",
    )(rows, gain, w1, b1, w2)
ENC_VMEM = 16
FIRST_VMEM = 34 * MIB


def project(rows, part_a, part_b, bias_ref, gain_ref, weight_ref):
    encoded = (
        rows[...].astype(F32) + (part_a[...].astype(F32) + part_b[...].astype(F32)) + bias_ref[...]
    )
    final = norm(encoded, gain_ref[1:2, :]).astype(BF16)
    return dot(final, weight_ref[...]).astype(BF16)


def project_kernel(rows, part_a, part_b, bias_ref, gain_ref, weight_ref, out_ref):
    out_ref[...] = project(rows, part_a, part_b, bias_ref, gain_ref, weight_ref)


def projection(rows, part_a, part_b, bias, gain, weight):
    return pl.pallas_call(
        project_kernel,
        in_specs=[WHOLE] * 6,
        out_specs=WHOLE,
        out_shape=jax.ShapeDtypeStruct((rows.shape[0], WIDTH), BF16),
        compiler_params=pltpu.CompilerParams(vmem_limit_bytes=16 * MIB),
        cost_estimate=pl.CostEstimate(
            flops=2 * rows.size * WIDTH, bytes_accessed=4 * MIB, transcendentals=0
        ),
        name="projection",
    )(rows, part_a, part_b, bias, gain, weight)


def handoff_kernel(seq_ref, pos_ref, own_ref, own_a, own_b, bias_ref, gain_ref, weight_ref,
                   peer_ref, out_ref):
    tokens = pos_ref.shape[1]
    own = project(own_ref, own_a, own_b, bias_ref, gain_ref, weight_ref)
    projected = jnp.concatenate([own, peer_ref[...]], axis=0)
    pos = pos_ref[...]
    chosen = ((pos >> 10) & 1) == seq_ref[0]
    clip_row = jnp.where(chosen, pos >> 11, -1).astype(F32)
    label_row = ((pos & (SPAN - 1)) + 1).astype(F32)
    down, across = iota((tokens, tokens), 0), iota((tokens, tokens), 1)
    same = down == across
    clip_col = jnp.sum(jnp.where(same, clip_row, 0.0), axis=1, keepdims=True)
    label_col = jnp.sum(jnp.where(same, label_row, 0.0), axis=1, keepdims=True)
    alike = clip_col == clip_row
    rank_col = jnp.sum(jnp.where(alike & (across < down), 1.0, 0.0), axis=1, keepdims=True)
    rank_row = jnp.sum(jnp.where(alike & (down < across), 1.0, 0.0), axis=0, keepdims=True)
    clips = out_ref.shape[0] // GROUP
    slot_row = jnp.where(clip_row >= 0, clip_row * GROUP + rank_row, -1.0).astype(jnp.int32)
    pick = (iota((clips * GROUP, tokens), 0) == slot_row).astype(F32).astype(BF16)
    packed = dot(pick, projected).astype(BF16).reshape(clips, GROUP, WIDTH)
    to_clip = (iota((clips, tokens), 0) == clip_row.astype(jnp.int32)).astype(F32).astype(BF16)
    upper = jnp.floor(label_col * (1.0 / 32.0))
    lower = label_col - 32.0 * upper
    lane = iota((tokens, 128), 1).astype(F32)
    codes = jnp.where(lane == rank_col, upper, 0.0) + jnp.where(lane == rank_col + 16.0, lower, 0.0)
    labels = dot(to_clip, codes.astype(BF16))
    first = jnp.where(
        iota((clips, GROUP, 128), 1) == LABEL_ROW,
        labels.reshape(clips, 1, 128),
        packed[:, :, :128].astype(F32),
    ).astype(BF16)
    out_ref[:, :128] = first.reshape(clips * GROUP, 128)
    out_ref[:, 128:] = packed[:, :, 128:].reshape(clips * GROUP, WIDTH - 128)


def handoff(seq, pos, own, own_a, own_b, bias, gain, weight, peer, clips):
    return pl.pallas_call(
        handoff_kernel,
        in_specs=[pl.BlockSpec(memory_space=pltpu.SMEM)] + [WHOLE] * 8,
        out_specs=WHOLE,
        out_shape=jax.ShapeDtypeStruct((clips * GROUP, WIDTH), BF16),
        compiler_params=pltpu.CompilerParams(vmem_limit_bytes=24 * MIB),
        cost_estimate=pl.CostEstimate(
            flops=2 * 512 * (704 * 512 + 1024 * 512), bytes_accessed=7 * MIB, transcendentals=0
        ),
        name="handoff",
    )(seq, pos, own, own_a, own_b, bias, gain, weight, peer)


def slot_labels(got_ref):
    slots = got_ref.shape[0]
    clips = slots // GROUP
    head = got_ref[:, :128].astype(F32).reshape(clips, GROUP, 128)
    codes = jnp.sum(jnp.where(iota(head.shape, 1) == LABEL_ROW, head, 0.0), axis=1)
    lane, place = iota((128, slots), 0), iota((128, slots), 1) % GROUP
    spread = jnp.where(lane == place, 32.0, 0.0) + jnp.where(lane == place + 16, 1.0, 0.0)
    by_clip = dot(codes.astype(BF16), spread.astype(BF16))
    mine = iota((clips, slots), 0) == iota((clips, slots), 1) // GROUP
    return jnp.sum(jnp.where(mine, by_clip, 0.0), axis=0, keepdims=True)


def stream_tile(half, first, count, got_ref, label_row, mask, parts):
    slots = got_ref.shape[0]
    want = (iota((count, slots), 0) + (first + 1)).astype(F32)
    place = (want == label_row).astype(F32)
    seen = jnp.sum(place, axis=1, keepdims=True)
    placed = dot(place.astype(BF16), got_ref[...])
    sin_a, cos_a, sin_b, cos_b = parts
    blocks = count // 32
    start = pl.multiple_of(half * (SPAN // 32) + first // 32, 8)
    coarse_sin = sin_a[pl.ds(start, blocks), :].reshape(blocks, 1, WIDTH)
    coarse_cos = cos_a[pl.ds(start, blocks), :].reshape(blocks, 1, WIDTH)
    table = coarse_sin * cos_b[...][None] + coarse_cos * sin_b[...][None]
    return placed + (1.0 - seen) * mask + table.reshape(count, WIDTH)


QKV_TILE = 512


def qkv_kernel(seq_ref, got_ref, sin_a, cos_a, sin_b, cos_b, mask_ref, gain_ref, weight_ref,
               bias_ref, stream_ref, query_ref, key_ref, value_ref):
    label_row = slot_labels(got_ref)
    scale = HEAD_D ** (-0.5) * math.log2(math.e)
    for first in range(0, SPAN, QKV_TILE):
        rows = pl.ds(first, QKV_TILE)
        stream = stream_tile(
            seq_ref[0], first, QKV_TILE, got_ref, label_row, mask_ref[...],
            (sin_a, cos_a, sin_b, cos_b),
        )
        stream_ref[rows, :] = stream
        normed = norm(stream, gain_ref[0:1, :]).astype(BF16)
        out = dot(normed, weight_ref[...]) + bias_ref[...]
        query_ref[rows, :] = (out[:, :WIDTH] * scale).astype(BF16)
        key_ref[rows, :] = out[:, WIDTH : 2 * WIDTH].astype(BF16)
        value_ref[:, rows] = out[:, 2 * WIDTH :].T.astype(BF16)


def own_qkv(seq, got, parts, mask, gain, weight, bias):
    return pl.pallas_call(
        qkv_kernel,
        in_specs=[pl.BlockSpec(memory_space=pltpu.SMEM)] + [WHOLE] * 9,
        out_specs=[WHOLE] * 4,
        out_shape=[
            jax.ShapeDtypeStruct((SPAN, WIDTH), F32),
            jax.ShapeDtypeStruct((SPAN, WIDTH), BF16),
            jax.ShapeDtypeStruct((SPAN, WIDTH), BF16),
            jax.ShapeDtypeStruct((WIDTH, SPAN), BF16),
        ],
        compiler_params=pltpu.CompilerParams(vmem_limit_bytes=20 * MIB),
        cost_estimate=pl.CostEstimate(
            flops=2 * SPAN * WIDTH * (3 * WIDTH + SPAN), bytes_accessed=9 * MIB, transcendentals=0
        ),
        name="own_qkv",
    )(seq, got, *parts, mask, gain, weight, bias)


ROW_TILE = 1024
FF_TILE = 512


def top(ref):
    head_of = (iota((WIDTH, 128), 0) // HEAD_D == iota((WIDTH, 128), 1)).astype(F32).astype(BF16)
    return jnp.max(dot(ref[...] * ref[...], head_of), axis=0, keepdims=True)


def is_safe(query_top, key_ref, value_ref):
    score_top = jnp.max(query_top * top(key_ref))
    value_top = jnp.max(jnp.abs(value_ref[...].astype(F32)))
    return (score_top <= SAFE * SAFE) & (value_top <= SAFE_VALUE)


def head_scores(query_ref, key_ref, pair, half):
    lanes = pl.ds(pl.multiple_of(pair * 128, 128), 128)
    query = query_ref[:, lanes]
    own_lane = (iota((1, 128), 1) < HEAD_D) == (half == 0)
    masked = jnp.where(own_lane, query, jnp.zeros_like(query))
    return lax.dot_general(
        key_ref[:, lanes], masked, (((1,), (1,)), ((), ())), preferred_element_type=F32
    )


def head_total(value_ref, weights, pair, half):
    value = value_ref[pl.ds(pl.multiple_of(pair * 128, 128), 128), :]
    own_row = (iota((128, 1), 0) < HEAD_D) == (half == 0)
    return dot(jnp.where(own_row, value, jnp.ones_like(value)), weights.astype(BF16))


def for_all_pairs(safe, attend):
    def run(peaked):
        def one_pair(pair, carry):
            attend(pair, peaked)
            return carry

        lax.fori_loop(0, HEADS // 2, one_pair, 0, unroll=1)

    pl.when(safe)(lambda: run(False))
    pl.when(jnp.logical_not(safe))(lambda: run(True))


def own_attention_kernel(query_ref, key_ref, value_ref, total_ref, shift_ref, top_ref, safe_ref):
    query_top = top(query_ref)
    top_ref[...] = query_top
    safe = is_safe(query_top, key_ref, value_ref)
    safe_ref[0] = safe.astype(jnp.int32)

    def attend(pair, peaked):
        for half in range(2):
            head = 2 * pair + half
            scores = head_scores(query_ref, key_ref, pair, half)
            if peaked:
                peak = jnp.max(scores, axis=0, keepdims=True)
                scores = scores - peak
                shift_ref[head] = peak
            else:
                shift_ref[head] = jnp.zeros((1, SPAN), F32)
            total_ref[head] = head_total(value_ref, jnp.exp2(scores), pair, half)

    for_all_pairs(safe, attend)


def own_attention(query, key, value):
    return pl.pallas_call(
        own_attention_kernel,
        in_specs=[WHOLE] * 3,
        out_specs=[WHOLE] * 3 + [pl.BlockSpec(memory_space=pltpu.SMEM)],
        out_shape=[
            jax.ShapeDtypeStruct((HEADS, 128, SPAN), F32),
            jax.ShapeDtypeStruct((HEADS, 1, SPAN), F32),
            jax.ShapeDtypeStruct((1, 128), F32),
            jax.ShapeDtypeStruct((1,), jnp.int32),
        ],
        compiler_params=pltpu.CompilerParams(vmem_limit_bytes=OWN_VMEM * MIB),
        cost_estimate=pl.CostEstimate(
            flops=16 * SPAN * SPAN * WIDTH,
            bytes_accessed=8 * MIB,
            transcendentals=HEADS * SPAN * SPAN,
        ),
        name="own_attention",
    )(query, key, value)


def decoder_kernel(safe_ref, query_ref, key_ref, value_ref, total_ref, shift_ref, top_ref,
                   stream_ref, gain_ref, out_weight_ref, out_bias_ref, fc1_ref, fc1_bias_ref,
                   fc2_ref, fc2_bias_ref, out_ref, attended, hidden):
    safe = (safe_ref[0] == 1) & is_safe(top_ref[...], key_ref, value_ref)

    def attend(pair, peaked):
        mixed = []
        for half in range(2):
            head = 2 * pair + half
            scores = head_scores(query_ref, key_ref, pair, half)
            before = total_ref[head]
            if peaked:
                shift = shift_ref[head]
                peak = jnp.maximum(shift, jnp.max(scores, axis=0, keepdims=True))
                scores = scores - peak
                before = before * jnp.exp2(shift - peak)
            mixed.append(before + head_total(value_ref, jnp.exp2(scores), pair, half))
        first = mixed[0][:HEAD_D] / mixed[0][HEAD_D:]
        second = mixed[1][HEAD_D:] / mixed[1][:HEAD_D]
        lanes = pl.ds(pl.multiple_of(pair * 128, 128), 128)
        attended[:, lanes] = jnp.concatenate([first, second], axis=0).T.astype(BF16)

    for_all_pairs(safe, attend)

    for first in range(0, SPAN, ROW_TILE):
        rows = pl.ds(first, ROW_TILE)
        stream2 = stream_ref[rows, :] + dot(attended[rows, :], out_weight_ref[...]) + out_bias_ref[...]
        normed2 = norm(stream2, gain_ref[1:2, :]).astype(BF16)
        for at in range(0, hidden.shape[1], FF_TILE):
            units = pl.ds(at, FF_TILE)
            inner = dot(normed2, fc1_ref[:, units]) + fc1_bias_ref[:, units]
            hidden[:, units] = gelu(inner).astype(BF16)
        out_ref[rows, :] = (stream2 + dot(hidden[...], fc2_ref[...]) + fc2_bias_ref[...]).astype(BF16)


def decoder(safe, *rest):
    fc1 = rest[-4]
    return pl.pallas_call(
        decoder_kernel,
        in_specs=[pl.BlockSpec(memory_space=pltpu.SMEM)] + [WHOLE] * len(rest),
        out_specs=WHOLE,
        out_shape=jax.ShapeDtypeStruct((SPAN, WIDTH), BF16),
        scratch_shapes=[
            pltpu.VMEM((SPAN, WIDTH), BF16),
            pltpu.VMEM((ROW_TILE, fc1.shape[1]), BF16),
        ],
        compiler_params=pltpu.CompilerParams(vmem_limit_bytes=DEC_VMEM * MIB),
        cost_estimate=pl.CostEstimate(
            flops=16 * SPAN * SPAN * WIDTH + 2 * SPAN * WIDTH * (WIDTH + 4096),
            bytes_accessed=16 * MIB,
            transcendentals=HEADS * SPAN * SPAN,
        ),
        name="decoder",
    )(safe, *rest)


OWN_VMEM = 18
DEC_VMEM = 24


def body(
    enc_rows,
    visible_pos,
    enc_norm_gain,
    enc_fc1,
    enc_fc1_bias,
    enc_fc2,
    enc_fc2_bias,
    handoff_weight,
    mask_token,
    dec_norm_gain,
    qkv_weight,
    qkv_bias,
    out_weight,
    out_bias,
    dec_fc1,
    dec_fc1_bias,
    dec_fc2,
    dec_fc2_bias,
):
    def swap(values):
        return lax.ppermute(values, "seq", [(0, 1), (1, 0)])

    def row(values):
        return values.reshape(1, -1)

    clips = lax.axis_size("rows")
    seq = lax.axis_index("seq").astype(jnp.int32).reshape(1)
    parts = tuple(jnp.asarray(part) for part in sinusoid_parts())
    bias1, bias2 = row(enc_fc1_bias), row(enc_fc2_bias)
    peer_rows = swap(enc_rows)
    peer_pos = swap(visible_pos)
    own_part, fc1_here, fc2_here = first_encoder_mlp(enc_rows, enc_norm_gain, enc_fc1, bias1, enc_fc2)
    peer_rows, peer_pos, own_part = lax.optimization_barrier((peer_rows, peer_pos, own_part))
    peer_part = second_encoder_mlp(peer_rows, enc_norm_gain, fc1_here, bias1, fc2_here)
    pos = jnp.concatenate([visible_pos, peer_pos]).reshape(1, -1)
    peer = projection(peer_rows, peer_part, swap(own_part), bias2, enc_norm_gain, handoff_weight)
    payload = handoff(
        seq, pos, enc_rows, own_part, swap(peer_part), bias2, enc_norm_gain, handoff_weight, peer, clips
    )
    mask, qkv_bias = row(mask_token), row(qkv_bias)
    payload, mask, qkv_bias = lax.optimization_barrier((payload, mask, qkv_bias))
    got = lax.all_to_all(
        payload.reshape(clips, GROUP, WIDTH), "rows", split_axis=0, concat_axis=0, tiled=True
    ).reshape(clips * GROUP, WIDTH)
    stream, query, key, value = own_qkv(
        seq, got, parts, mask, dec_norm_gain, qkv_weight, qkv_bias
    )
    peer_key, peer_value = swap(key), swap(value)
    total, shift, query_top, safe = own_attention(query, key, value)
    decoded = decoder(
        safe, query, peer_key, peer_value, total, shift, query_top, stream, dec_norm_gain,
        out_weight, row(out_bias), dec_fc1, row(dec_fc1_bias), dec_fc2, row(dec_fc2_bias),
    )
    return decoded.reshape(1, SPAN, WIDTH)


def solution(mesh):
    return jax.shard_map(
        body,
        mesh=mesh,
        in_specs=(
            P(("rows", "seq"), None),
            P(("rows", "seq")),
            P(),
            P(None, "seq"),
            P("seq"),
            P("seq", None),
            P(),
            P(),
            P(),
            P(),
            P(),
            P(),
            P(),
            P(),
            P(),
            P(),
            P(),
            P(),
        ),
        out_specs=P("rows", "seq", None),
        check_vma=False,
    )
```

profile of v0, /device:TPU:1, one launch (start us, length us, event | category | flops | bytes accessed | tf_op | source)
XLA Modules:
  0.0 97.1 jit_solution(4804717895058274510)
XLA Ops:
  0.0 1.4 %collective-permute-start = (bf16[256,1408]{1,0:T(8,128)(2,1)}, bf16[256,1408]{1,0:T(8,128)(2,1)S(1)}, u32[]{:S(2)}, u32[]{:S(2)}) collective-permute-start(bf16[256,1408]{1,0:T(8,128)(2,1)} %own_ref.1), channel_id=1, source_target_pairs={{0,1},{1,0},{2,3},{3,2},{4,5},{5,4},{6,7},{7,6},{8,9},{9,8},{10,11... | collective-permute-start | bytes 2162696 | tf_op jit(solution)/shard_map/ppermute | solution.py:475
  1.4 1.1 %copy-done.1 = bf16[256,1408]{1,0:T(8,128)(2,1)S(1)} copy-done((bf16[256,1408]{1,0:T(8,128)(2,1)S(1)}, bf16[256,1408]{1,0:T(8,128)(2,1)}, u32[]{:S(2)}) %copy-start.1) | copy-done | bytes 720920
  2.5 0.7 copy-done.3
  3.2 0.7 copy-done.5
  3.9 10.1 %first_encoder_mlp.1 = (bf16[256,1408]{1,0:T(8,128)(2,1)}, bf16[1408,3072]{1,0:T(8,128)(2,1)S(1)}, bf16[3072,1408]{1,0:T(8,128)(2,1)S(1)}) custom-call(bf16[256,1408]{1,0:T(8,128)(2,1)S(1)} %copy-done.1, f32[2,1408]{1,0:T(2,128)S(1)} %copy-done.3, bf16[1408,3072]{1,0:T(8,128)(2,1)} %w1_ref.1, f32[1,3072]{1,0:T(1,128)S(1)} %bitcast.12, bf16[3072,1408]{1,0:T(8,128)(2,1)} %w2_ref.1), custom_call_target="tpu_custom_call" | custom-call | flops 4429185024 | bytes 18743296 | tf_op jit(solution)/shard_map/first_encoder_mlp/pallas_call | solution.py:117
  14.1 0.6 collective-permute-start.3
  14.7 0.0 copy-start.4
  14.7 6.5 %second_encoder_mlp.1.part_a = bf16[256,1408]{1,0:T(8,128)(2,1)} custom-call(bf16[256,1408]{1,0:T(8,128)(2,1)S(1)} %collective-permute-done.rows_ref.rows, f32[2,1408]{1,0:T(2,128)S(1)} %copy-done.3, bf16[1408,3072]{1,0:T(8,128)(2,1)S(1)} %get-tuple-element.26.w1, f32[1,3072]{1,0:T(1,128)S(1)} %bitcast.13, bf16[3072,1408]{1,0:T(8,128)(2,1)S(1)} %get-tuple-element.27.w2), custom_call_target="tpu_custom_call" | custom-call | flops 4429185024 | bytes 18743296 | tf_op jit(solution)/shard_map/second_encoder_mlp/pallas_call | solution.py:153
  21.2 0.1 collective-permute-start.2
  21.3 2.5 %projection.1.peer_ref = bf16[256,512]{1,0:T(8,128)(2,1)S(1)} custom-call(bf16[256,1408]{1,0:T(8,128)(2,1)S(1)} %collective-permute-done.rows_ref.rows, bf16[256,1408]{1,0:T(8,128)(2,1)} %second_encoder_mlp.1.part_a, bf16[256,1408]{1,0:T(8,128)(2,1)} %collective-permute-done.3.part_b, f32[1,1408]{1,0:T(1,128)S(1)} %reshape.39.bias_ref, ...), custom_call_target="tpu_custom_call" | custom-call | flops 369098752 | bytes 4194304 | tf_op jit(solution)/shard_map/projection/pallas_call | solution.py:180
  23.8 0.0 copy-start.8
  23.8 0.0 copy-start.11
  23.9 0.0 copy-start.12
  23.9 0.0 copy-start.15
  23.9 0.0 copy-start.16
  23.9 0.0 copy-start.17
  23.9 0.0 copy-start.18
  23.9 3.3 %handoff.1 = bf16[1024,512]{1,0:T(8,128)(2,1)S(1)} custom-call(s32[1]{0:T(128)} %bitcast.seq_ref, s32[1,512]{1,0:T(1,128)S(1)} %bitcast.14, bf16[256,1408]{1,0:T(8,128)(2,1)S(1)} %copy-done.2, bf16[256,1408]{1,0:T(8,128)(2,1)} %get-tuple-element.24.own_a, bf16[256,1408]{1,0:T(8,128)(2,1)} %collective-permute-done.2.own_b, f32[1,1408]{1,0:T(1,128)S(1)} %reshape.39.bias_ref, ...), custom_call_target="tpu_custom_call" | custom-call | flops 905969664 | bytes 7340032 | tf_op jit(solution)/shard_map/handoff/pallas_call | solution.py:229
  27.3 29.1 %all_to_all.5 = bf16[64,16,512]{2,1,0:T(8,128)(2,1)S(1)} all-to-all(bf16[64,16,512]{2,1,0:T(8,128)(2,1)S(1)} %bitcast.10), channel_id=1, replica_groups=mesh['rows'=64,'seq'=2] {'rows'}, dimensions={0} | all-to-all | bytes 2097152 | tf_op jit(solution)/shard_map/all_to_all | solution.py:496
  56.4 4.2 %own_qkv.1 = (f32[1024,512]{1,0:T(8,128)S(1)}, bf16[1024,512]{1,0:T(8,128)(2,1)S(1)}, bf16[1024,512]{1,0:T(8,128)(2,1)S(1)}, bf16[512,1024]{1,0:T(8,128)(2,1)S(1)}) custom-call(s32[1]{0:T(128)} %bitcast.seq_ref, bf16[1024,512]{1,0:T(8,128)(2,1)S(1)} %bitcast.11, f32[64,512]{1,0:T(8,128)S(1)} %copy-done.15, f32[64,512]{1,0:T(8,128)S(1)} %copy-done.16, ...), custom_call_target="tpu_custom_call" | custom-call | flops 2684354560 | bytes 9437184 | tf_op jit(solution)/shard_map/own_qkv/pallas_call | solution.py:291
  60.6 1.8 %collective-permute-start.4 = (bf16[1024,512]{1,0:T(8,128)(2,1)S(1)}, bf16[1024,512]{1,0:T(8,128)(2,1)S(1)}, u32[]{:S(2)}, u32[]{:S(2)}) collective-permute-start(bf16[1024,512]{1,0:T(8,128)(2,1)S(1)} %get-tuple-element.32.key_ref), channel_id=1, source_target_pairs={{0,1},{1,0},{2,3},{3,2},{4,5},{5,4},{6,7},{7,6},{8,9},{9,8},{10,11... | collective-permute-start | bytes 3145736 | tf_op jit(solution)/shard_map/ppermute | solution.py:475
  62.5 0.1 collective-permute-start.5
  62.6 13.1 %own_attention.1 = (f32[8,128,1024]{2,1,0:T(8,128)S(1)}, f32[8,1,1024]{2,1,0:T(1,128)S(1)}, f32[1,128]{1,0:T(1,128)S(1)}, s32[1]{0:T(128)}) custom-call(bf16[1024,512]{1,0:T(8,128)(2,1)S(1)} %get-tuple-element.31.query_ref, bf16[1024,512]{1,0:T(8,128)(2,1)S(1)} %get-tuple-element.32.key_ref, bf16[512,1024]{1,0:T(8,128)(2,1)S(1)} %get-tuple-element.33.value_ref), custom_call_target="tpu_custom_call" | custom-call | flops 8589934592 | bytes 8388608 | tf_op jit(solution)/shard_map/own_attention/pallas_call | solution.py:374
  75.7 21.4 %decoder.1 = bf16[1024,512]{1,0:T(8,128)(2,1)} custom-call(s32[1]{0:T(128)} %get-tuple-element.34.safe_ref, bf16[1024,512]{1,0:T(8,128)(2,1)S(1)} %get-tuple-element.31.query_ref, bf16[1024,512]{1,0:T(8,128)(2,1)S(1)} %collective-permute-done.4.key_ref, bf16[512,1024]{1,0:T(8,128)(2,1)S(1)} %collective-permute-done.5.value_ref, ...), custom_call_target="tpu_custom_call" | custom-call | flops 13421772800 | bytes 16777216 | tf_op jit(solution)/shard_map/decoder/pallas_call | solution.py:431
  (43 shorter events, 0.1 us)
Async XLA Ops:
  0.0 14.1 %collective-permute-start = (bf16[256,1408]{1,0:T(8,128)(2,1)}, bf16[256,1408]{1,0:T(8,128)(2,1)S(1)}, u32[]{:S(2)}, u32[]{:S(2)}) collective-permute-start(bf16[256,1408]{1,0:T(8,128)(2,1)} %own_ref.1), channel_id=1, source_target_pairs={{0,1},{1,0},{2,3},{3,2},{4,5},{5,4},{6,7},{7,6},{8,9},{9,8},{10,11... | collective-permute-start | bytes 2162696 | tf_op jit(solution)/shard_map/ppermute | solution.py:475
  1.4 12.6 %collective-permute-start.1 = (s32[256]{0:T(256)}, s32[256]{0:T(256)S(1)}, u32[]{:S(2)}, u32[]{:S(2)}) collective-permute-start(s32[256]{0:T(256)} %param.23), channel_id=1, source_target_pairs={{0,1},{1,0},{2,3},{3,2},{4,5},{5,4},{6,7},{7,6},{8,9},{9,8},{10,11... | collective-permute-start | bytes 3080 | tf_op jit(solution)/shard_map/ppermute | solution.py:475
  14.1 7.2 %collective-permute-start.3 = (bf16[256,1408]{1,0:T(8,128)(2,1)}, bf16[256,1408]{1,0:T(8,128)(2,1)}, u32[]{:S(2)}, u32[]{:S(2)}) collective-permute-start(bf16[256,1408]{1,0:T(8,128)(2,1)} %get-tuple-element.24.own_a), channel_id=1, source_target_pairs={{0,1},{1,0},{2,3},{3,2},{4,5},{5,4},{6,7},{7,6},{8,9},{9,8},{10,11... | collective-permute-start | bytes 2162696 | tf_op jit(solution)/shard_map/ppermute | solution.py:475
  14.7 6.6 %copy-start.19 = (f32[1408]{0:T(1024)S(1)}, f32[1408]{0:T(1024)}, u32[]{:S(2)}) copy-start(f32[1408]{0:T(1024)} %param.28) | copy-start | bytes 16900
  14.7 6.6 %copy-start.20 = (f32[1536]{0:T(1024)S(1)}, f32[1536]{0:T(1024)}, u32[]{:S(2)}) copy-start(f32[1536]{0:T(1024)} %param.33) | copy-start | bytes 18436
  14.7 6.6 %copy-start.21 = (s32[256]{0:T(256)S(1)}, s32[256]{0:T(256)}, u32[]{:S(2)}) copy-start(s32[256]{0:T(256)} %param.23) | copy-start | bytes 3076
  14.7 6.6 %copy-start = (bf16[1408,512]{1,0:T(8,128)(2,1)S(1)}, bf16[1408,512]{1,0:T(8,128)(2,1)}, u32[]{:S(2)}) copy-start(bf16[1408,512]{1,0:T(8,128)(2,1)} %weight_ref.4) | copy-start | bytes 4325380
  14.7 6.6 %copy-start.4 = (f32[2,1408]{1,0:T(2,128)S(1)}, f32[2,1408]{1,0:T(2,128)}, u32[]{:S(2)}) copy-start(f32[2,1408]{1,0:T(2,128)} %gain_ref.9) | copy-start | bytes 33796
  21.2 2.7 %collective-permute-start.2 = (bf16[256,1408]{1,0:T(8,128)(2,1)}, bf16[256,1408]{1,0:T(8,128)(2,1)}, u32[]{:S(2)}, u32[]{:S(2)}) collective-permute-start(bf16[256,1408]{1,0:T(8,128)(2,1)} %second_encoder_mlp.1.part_a), channel_id=1, source_target_pairs={{0,1},{1,0},{2,3},{3,2},{4,5},{5,4},{6,7},{7,6},{8,9},{9,8},{10,11... | collective-permute-start | bytes 2162696 | tf_op jit(solution)/shard_map/ppermute | solution.py:475
  23.8 32.5 %copy-start.8 = (bf16[512,1536]{1,0:T(8,128)(2,1)S(1)}, bf16[512,1536]{1,0:T(8,128)(2,1)}, u32[]{:S(2)}) copy-start(bf16[512,1536]{1,0:T(8,128)(2,1)} %weight_ref.5) | copy-start | bytes 4718596
  23.8 32.5 %copy-start.11 = (f32[2,512]{1,0:T(2,128)S(1)}, f32[2,512]{1,0:T(2,128)}, u32[]{:S(2)}) copy-start(f32[2,512]{1,0:T(2,128)} %gain_ref.11) | copy-start | bytes 12292
  23.9 32.5 %copy-start.12 = (f32[512]{0:T(512)S(1)}, f32[512]{0:T(512)}, u32[]{:S(2)}) copy-start(f32[512]{0:T(512)} %param.30) | copy-start | bytes 6148
  23.9 32.5 %copy-start.15 = (f32[64,512]{1,0:T(8,128)S(1)}, f32[64,512]{1,0:T(8,128)}, u32[]{:S(2)}) copy-start(f32[64,512]{1,0:T(8,128)} %constant.12.clone.sin_a) | copy-start | bytes 393220
  23.9 32.5 %copy-start.16 = (f32[64,512]{1,0:T(8,128)S(1)}, f32[64,512]{1,0:T(8,128)}, u32[]{:S(2)}) copy-start(f32[64,512]{1,0:T(8,128)} %constant.13.clone.cos_a) | copy-start | bytes 393220
  23.9 32.5 %copy-start.17 = (f32[32,512]{1,0:T(8,128)S(1)}, f32[32,512]{1,0:T(8,128)}, u32[]{:S(2)}) copy-start(f32[32,512]{1,0:T(8,128)} %constant.14.clone.sin_b) | copy-start | bytes 196612
  23.9 32.5 %copy-start.18 = (f32[32,512]{1,0:T(8,128)S(1)}, f32[32,512]{1,0:T(8,128)}, u32[]{:S(2)}) copy-start(f32[32,512]{1,0:T(8,128)} %constant.15.clone.cos_b) | copy-start | bytes 196612
  60.6 15.0 %collective-permute-start.4 = (bf16[1024,512]{1,0:T(8,128)(2,1)S(1)}, bf16[1024,512]{1,0:T(8,128)(2,1)S(1)}, u32[]{:S(2)}, u32[]{:S(2)}) collective-permute-start(bf16[1024,512]{1,0:T(8,128)(2,1)S(1)} %get-tuple-element.32.key_ref), channel_id=1, source_target_pairs={{0,1},{1,0},{2,3},{3,2},{4,5},{5,4},{6,7},{7,6},{8,9},{9,8},{10,11... | collective-permute-start | bytes 3145736 | tf_op jit(solution)/shard_map/ppermute | solution.py:475
  62.5 13.2 %collective-permute-start.5 = (bf16[512,1024]{1,0:T(8,128)(2,1)S(1)}, bf16[512,1024]{1,0:T(8,128)(2,1)S(1)}, u32[]{:S(2)}, u32[]{:S(2)}) collective-permute-start(bf16[512,1024]{1,0:T(8,128)(2,1)S(1)} %get-tuple-element.33.value_ref), channel_id=1, source_target_pairs={{0,1},{1,0},{2,3},{3,2},{4,5},{5,4},{6,7},{7,6},{8,9},{9,8},{10,11... | collective-permute-start | bytes 3145736 | tf_op jit(solution)/shard_map/ppermute | solution.py:475
  62.6 13.1 %copy-start.6 = (bf16[512,2048]{1,0:T(8,128)(2,1)S(1)}, bf16[512,2048]{1,0:T(8,128)(2,1)}, u32[]{:S(2)}) copy-start(bf16[512,2048]{1,0:T(8,128)(2,1)} %fc1_ref.1) | copy-start | bytes 6291460
  62.6 13.1 %copy-start.7 = (bf16[2048,512]{1,0:T(8,128)(2,1)S(1)}, bf16[2048,512]{1,0:T(8,128)(2,1)}, u32[]{:S(2)}) copy-start(bf16[2048,512]{1,0:T(8,128)(2,1)} %fc2_ref.1) | copy-start | bytes 6291460
  62.6 13.1 %copy-start.9 = (bf16[512,512]{1,0:T(8,128)(2,1)S(1)}, bf16[512,512]{1,0:T(8,128)(2,1)}, u32[]{:S(2)}) copy-start(bf16[512,512]{1,0:T(8,128)(2,1)} %out_weight_ref.1) | copy-start | bytes 1572868
  62.6 13.1 %copy-start.10 = (f32[2048]{0:T(1024)S(1)}, f32[2048]{0:T(1024)}, u32[]{:S(2)}) copy-start(f32[2048]{0:T(1024)} %param.37) | copy-start | bytes 24580
  62.6 13.2 %copy-start.13 = (f32[512]{0:T(512)S(1)}, f32[512]{0:T(512)}, u32[]{:S(2)}) copy-start(f32[512]{0:T(512)} %param.35) | copy-start | bytes 6148
  62.6 13.1 %copy-start.14 = (f32[512]{0:T(512)S(1)}, f32[512]{0:T(512)}, u32[]{:S(2)}) copy-start(f32[512]{0:T(512)} %param.39) | copy-start | bytes 6148
  (4 other events, 5.3 us)
where the time goes:
time: 97.4 us; the launch traced here: 97.1 us
  Pallas kernels  61 us (63%)
  blocking collectives  29.1 us (30%)
  starting transfers between devices  4 us (4%)
  local copies, waits for them, and re-layouts  2.63 us (3%)
    all_to_all x1, blocking collectives, body(): lax.all_to_all(payload.reshape(clips, GROUP, WIDTH), 'rows', split_axis=0...  29.1 us
    pallas_call x1, Pallas kernels, decoder(): pl.pallas_call(decoder_kernel, in_specs=[pl.BlockSpec(memory_space=pltpu....  21.4 us
    pallas_call x1, Pallas kernels, own_attention(): pl.pallas_call(own_attention_kernel, in_specs=[WHOLE] * 3, out_specs=[WHO...  13.1 us
    pallas_call x1, Pallas kernels, first_encoder_mlp(): pl.pallas_call(enc_kernel, in_specs=[far] * 5, out_specs=[WHOLE] * 3, out...  10.1 us
    pallas_call x1, Pallas kernels, second_encoder_mlp(): pl.pallas_call(second_enc_kernel, in_specs=[WHOLE] * 5, out_specs=WHOLE,...  6.5 us
    pallas_call x1, Pallas kernels, own_qkv(): pl.pallas_call(qkv_kernel, in_specs=[pl.BlockSpec(memory_space=pltpu.SMEM...  4.19 us
    ppermute x6, starting transfers between devices, swap(): return lax.ppermute(values, 'seq', [(0, 1), (1, 0)])  4 us
    pallas_call x1, Pallas kernels, handoff(): pl.pallas_call(handoff_kernel, in_specs=[pl.BlockSpec(memory_space=pltpu....  3.33 us
  transfers between devices with their start and end apart: 6, of which 0 were waited for; matrix products, arithmetic and copies ran while one was open for 0% of the time, Pallas kernels for 33%

commit v1 on v0

--- a/solution.py
+++ b/solution.py
@@ -317,7 +317,11 @@
 
 def is_safe(query_top, key_ref, value_ref):
     score_top = jnp.max(query_top * top(key_ref))
-    value_top = jnp.max(jnp.abs(value_ref[...].astype(F32)))
+    sizes = jnp.abs(value_ref[...])
+    while sizes.shape[0] > 16:
+        middle = sizes.shape[0] // 2
+        sizes = jnp.maximum(sizes[:middle], sizes[middle:])
+    value_top = jnp.max(sizes.astype(F32))
     return (score_top <= SAFE * SAFE) & (value_top <= SAFE_VALUE)
 
 

time: 97.4 us -> 97.4 us (level)
  no operation moved by 1% of the time
where the time goes in v1:
time: 97.4 us; the launch traced here: 97 us
  Pallas kernels  61 us (63%)
  blocking collectives  29.1 us (30%)
  starting transfers between devices  4 us (4%)
  local copies, waits for them, and re-layouts  2.63 us (3%)
    all_to_all x1, blocking collectives, body(): lax.all_to_all(payload.reshape(clips, GROUP, WIDTH), 'rows', split_axis=0...  29.1 us
    pallas_call x1, Pallas kernels, decoder(): pl.pallas_call(decoder_kernel, in_specs=[pl.BlockSpec(memory_space=pltpu....  21.4 us
    pallas_call x1, Pallas kernels, own_attention(): pl.pallas_call(own_attention_kernel, in_specs=[WHOLE] * 3, out_specs=[WHO...  13 us
    pallas_call x1, Pallas kernels, first_encoder_mlp(): pl.pallas_call(enc_kernel, in_specs=[far] * 5, out_specs=[WHOLE] * 3, out...  10.1 us
    pallas_call x1, Pallas kernels, second_encoder_mlp(): pl.pallas_call(second_enc_kernel, in_specs=[WHOLE] * 5, out_specs=WHOLE,...  6.5 us
    pallas_call x1, Pallas kernels, own_qkv(): pl.pallas_call(qkv_kernel, in_specs=[pl.BlockSpec(memory_space=pltpu.SMEM...  4.19 us
    ppermute x6, starting transfers between devices, swap(): return lax.ppermute(values, 'seq', [(0, 1), (1, 0)])  4 us
    pallas_call x1, Pallas kernels, handoff(): pl.pallas_call(handoff_kernel, in_specs=[pl.BlockSpec(memory_space=pltpu....  3.33 us
  transfers between devices with their start and end apart: 6, of which 0 were waited for; matrix products, arithmetic and copies ran while one was open for 0% of the time, Pallas kernels for 33%

profile of v1, /device:TPU:1, one launch (start us, length us, event | category | flops | bytes accessed | tf_op | source)
XLA Modules:
  0.0 97.0 jit_solution(11045790310334077905)
XLA Ops:
  0.0 1.4 %collective-permute-start = (bf16[256,1408]{1,0:T(8,128)(2,1)}, bf16[256,1408]{1,0:T(8,128)(2,1)S(1)}, u32[]{:S(2)}, u32[]{:S(2)}) collective-permute-start(bf16[256,1408]{1,0:T(8,128)(2,1)} %own_ref.1), channel_id=1, source_target_pairs={{0,1},{1,0},{2,3},{3,2},{4,5},{5,4},{6,7},{7,6},{8,9},{9,8},{10,11... | collective-permute-start | bytes 2162696 | tf_op jit(solution)/shard_map/ppermute | solution.py:479
  1.4 1.1 %copy-done.1 = bf16[256,1408]{1,0:T(8,128)(2,1)S(1)} copy-done((bf16[256,1408]{1,0:T(8,128)(2,1)S(1)}, bf16[256,1408]{1,0:T(8,128)(2,1)}, u32[]{:S(2)}) %copy-start.1) | copy-done | bytes 720920
  2.5 0.7 copy-done.3
  3.2 0.7 copy-done.5
  3.9 10.1 %first_encoder_mlp.1 = (bf16[256,1408]{1,0:T(8,128)(2,1)}, bf16[1408,3072]{1,0:T(8,128)(2,1)S(1)}, bf16[3072,1408]{1,0:T(8,128)(2,1)S(1)}) custom-call(bf16[256,1408]{1,0:T(8,128)(2,1)S(1)} %copy-done.1, f32[2,1408]{1,0:T(2,128)S(1)} %copy-done.3, bf16[1408,3072]{1,0:T(8,128)(2,1)} %w1_ref.1, f32[1,3072]{1,0:T(1,128)S(1)} %bitcast.12, bf16[3072,1408]{1,0:T(8,128)(2,1)} %w2_ref.1), custom_call_target="tpu_custom_call" | custom-call | flops 4429185024 | bytes 18743296 | tf_op jit(solution)/shard_map/first_encoder_mlp/pallas_call | solution.py:117
  14.1 0.6 collective-permute-start.3
  14.7 0.0 copy-start.4
  14.7 6.5 %second_encoder_mlp.1.part_a = bf16[256,1408]{1,0:T(8,128)(2,1)} custom-call(bf16[256,1408]{1,0:T(8,128)(2,1)S(1)} %collective-permute-done.rows_ref.rows, f32[2,1408]{1,0:T(2,128)S(1)} %copy-done.3, bf16[1408,3072]{1,0:T(8,128)(2,1)S(1)} %get-tuple-element.26.w1, f32[1,3072]{1,0:T(1,128)S(1)} %bitcast.13, bf16[3072,1408]{1,0:T(8,128)(2,1)S(1)} %get-tuple-element.27.w2), custom_call_target="tpu_custom_call" | custom-call | flops 4429185024 | bytes 18743296 | tf_op jit(solution)/shard_map/second_encoder_mlp/pallas_call | solution.py:153
  21.2 0.1 collective-permute-start.2
  21.3 2.5 %projection.1.peer_ref = bf16[256,512]{1,0:T(8,128)(2,1)S(1)} custom-call(bf16[256,1408]{1,0:T(8,128)(2,1)S(1)} %collective-permute-done.rows_ref.rows, bf16[256,1408]{1,0:T(8,128)(2,1)} %second_encoder_mlp.1.part_a, bf16[256,1408]{1,0:T(8,128)(2,1)} %collective-permute-done.3.part_b, f32[1,1408]{1,0:T(1,128)S(1)} %reshape.39.bias_ref, ...), custom_call_target="tpu_custom_call" | custom-call | flops 369098752 | bytes 4194304 | tf_op jit(solution)/shard_map/projection/pallas_call | solution.py:180
  23.8 0.0 copy-start.8
  23.8 0.0 copy-start.11
  23.9 0.0 copy-start.12
  23.9 0.0 copy-start.15
  23.9 0.0 copy-start.16
  23.9 0.0 copy-start.17
  23.9 0.0 copy-start.18
  23.9 3.3 %handoff.1 = bf16[1024,512]{1,0:T(8,128)(2,1)S(1)} custom-call(s32[1]{0:T(128)} %bitcast.seq_ref, s32[1,512]{1,0:T(1,128)S(1)} %bitcast.14, bf16[256,1408]{1,0:T(8,128)(2,1)S(1)} %copy-done.2, bf16[256,1408]{1,0:T(8,128)(2,1)} %get-tuple-element.24.own_a, bf16[256,1408]{1,0:T(8,128)(2,1)} %collective-permute-done.2.own_b, f32[1,1408]{1,0:T(1,128)S(1)} %reshape.39.bias_ref, ...), custom_call_target="tpu_custom_call" | custom-call | flops 905969664 | bytes 7340032 | tf_op jit(solution)/shard_map/handoff/pallas_call | solution.py:229
  27.3 29.1 %all_to_all.5 = bf16[64,16,512]{2,1,0:T(8,128)(2,1)S(1)} all-to-all(bf16[64,16,512]{2,1,0:T(8,128)(2,1)S(1)} %bitcast.10), channel_id=1, replica_groups=mesh['rows'=64,'seq'=2] {'rows'}, dimensions={0} | all-to-all | bytes 2097152 | tf_op jit(solution)/shard_map/all_to_all | solution.py:500
  56.4 4.2 %own_qkv.1 = (f32[1024,512]{1,0:T(8,128)S(1)}, bf16[1024,512]{1,0:T(8,128)(2,1)S(1)}, bf16[1024,512]{1,0:T(8,128)(2,1)S(1)}, bf16[512,1024]{1,0:T(8,128)(2,1)S(1)}) custom-call(s32[1]{0:T(128)} %bitcast.seq_ref, bf16[1024,512]{1,0:T(8,128)(2,1)S(1)} %bitcast.11, f32[64,512]{1,0:T(8,128)S(1)} %copy-done.15, f32[64,512]{1,0:T(8,128)S(1)} %copy-done.16, ...), custom_call_target="tpu_custom_call" | custom-call | flops 2684354560 | bytes 9437184 | tf_op jit(solution)/shard_map/own_qkv/pallas_call | solution.py:291
  60.6 1.8 %collective-permute-start.4 = (bf16[1024,512]{1,0:T(8,128)(2,1)S(1)}, bf16[1024,512]{1,0:T(8,128)(2,1)S(1)}, u32[]{:S(2)}, u32[]{:S(2)}) collective-permute-start(bf16[1024,512]{1,0:T(8,128)(2,1)S(1)} %get-tuple-element.32.key_ref), channel_id=1, source_target_pairs={{0,1},{1,0},{2,3},{3,2},{4,5},{5,4},{6,7},{7,6},{8,9},{9,8},{10,11... | collective-permute-start | bytes 3145736 | tf_op jit(solution)/shard_map/ppermute | solution.py:479
  62.5 0.1 collective-permute-start.5
  62.6 13.0 %own_attention.1 = (f32[8,128,1024]{2,1,0:T(8,128)S(1)}, f32[8,1,1024]{2,1,0:T(1,128)S(1)}, f32[1,128]{1,0:T(1,128)S(1)}, s32[1]{0:T(128)}) custom-call(bf16[1024,512]{1,0:T(8,128)(2,1)S(1)} %get-tuple-element.31.query_ref, bf16[1024,512]{1,0:T(8,128)(2,1)S(1)} %get-tuple-element.32.key_ref, bf16[512,1024]{1,0:T(8,128)(2,1)S(1)} %get-tuple-element.33.value_ref), custom_call_target="tpu_custom_call" | custom-call | flops 8589934592 | bytes 8388608 | tf_op jit(solution)/shard_map/own_attention/pallas_call | solution.py:378
  75.7 21.4 %decoder.1 = bf16[1024,512]{1,0:T(8,128)(2,1)} custom-call(s32[1]{0:T(128)} %get-tuple-element.34.safe_ref, bf16[1024,512]{1,0:T(8,128)(2,1)S(1)} %get-tuple-element.31.query_ref, bf16[1024,512]{1,0:T(8,128)(2,1)S(1)} %collective-permute-done.4.key_ref, bf16[512,1024]{1,0:T(8,128)(2,1)S(1)} %collective-permute-done.5.value_ref, ...), custom_call_target="tpu_custom_call" | custom-call | flops 13421772800 | bytes 16777216 | tf_op jit(solution)/shard_map/decoder/pallas_call | solution.py:435
  (43 shorter events, 0.1 us)
Async XLA Ops:
  0.0 14.1 %collective-permute-start = (bf16[256,1408]{1,0:T(8,128)(2,1)}, bf16[256,1408]{1,0:T(8,128)(2,1)S(1)}, u32[]{:S(2)}, u32[]{:S(2)}) collective-permute-start(bf16[256,1408]{1,0:T(8,128)(2,1)} %own_ref.1), channel_id=1, source_target_pairs={{0,1},{1,0},{2,3},{3,2},{4,5},{5,4},{6,7},{7,6},{8,9},{9,8},{10,11... | collective-permute-start | bytes 2162696 | tf_op jit(solution)/shard_map/ppermute | solution.py:479
  1.4 12.6 %collective-permute-start.1 = (s32[256]{0:T(256)}, s32[256]{0:T(256)S(1)}, u32[]{:S(2)}, u32[]{:S(2)}) collective-permute-start(s32[256]{0:T(256)} %param.23), channel_id=1, source_target_pairs={{0,1},{1,0},{2,3},{3,2},{4,5},{5,4},{6,7},{7,6},{8,9},{9,8},{10,11... | collective-permute-start | bytes 3080 | tf_op jit(solution)/shard_map/ppermute | solution.py:479
  14.1 7.2 %collective-permute-start.3 = (bf16[256,1408]{1,0:T(8,128)(2,1)}, bf16[256,1408]{1,0:T(8,128)(2,1)}, u32[]{:S(2)}, u32[]{:S(2)}) collective-permute-start(bf16[256,1408]{1,0:T(8,128)(2,1)} %get-tuple-element.24.own_a), channel_id=1, source_target_pairs={{0,1},{1,0},{2,3},{3,2},{4,5},{5,4},{6,7},{7,6},{8,9},{9,8},{10,11... | collective-permute-start | bytes 2162696 | tf_op jit(solution)/shard_map/ppermute | solution.py:479
  14.7 6.6 %copy-start.19 = (f32[1408]{0:T(1024)S(1)}, f32[1408]{0:T(1024)}, u32[]{:S(2)}) copy-start(f32[1408]{0:T(1024)} %param.28) | copy-start | bytes 16900
  14.7 6.6 %copy-start.20 = (f32[1536]{0:T(1024)S(1)}, f32[1536]{0:T(1024)}, u32[]{:S(2)}) copy-start(f32[1536]{0:T(1024)} %param.33) | copy-start | bytes 18436
  14.7 6.6 %copy-start.21 = (s32[256]{0:T(256)S(1)}, s32[256]{0:T(256)}, u32[]{:S(2)}) copy-start(s32[256]{0:T(256)} %param.23) | copy-start | bytes 3076
  14.7 6.6 %copy-start = (bf16[1408,512]{1,0:T(8,128)(2,1)S(1)}, bf16[1408,512]{1,0:T(8,128)(2,1)}, u32[]{:S(2)}) copy-start(bf16[1408,512]{1,0:T(8,128)(2,1)} %weight_ref.4) | copy-start | bytes 4325380
  14.7 6.6 %copy-start.4 = (f32[2,1408]{1,0:T(2,128)S(1)}, f32[2,1408]{1,0:T(2,128)}, u32[]{:S(2)}) copy-start(f32[2,1408]{1,0:T(2,128)} %gain_ref.9) | copy-start | bytes 33796
  21.2 2.7 %collective-permute-start.2 = (bf16[256,1408]{1,0:T(8,128)(2,1)}, bf16[256,1408]{1,0:T(8,128)(2,1)}, u32[]{:S(2)}, u32[]{:S(2)}) collective-permute-start(bf16[256,1408]{1,0:T(8,128)(2,1)} %second_encoder_mlp.1.part_a), channel_id=1, source_target_pairs={{0,1},{1,0},{2,3},{3,2},{4,5},{5,4},{6,7},{7,6},{8,9},{9,8},{10,11... | collective-permute-start | bytes 2162696 | tf_op jit(solution)/shard_map/ppermute | solution.py:479
  23.8 32.5 %copy-start.8 = (bf16[512,1536]{1,0:T(8,128)(2,1)S(1)}, bf16[512,1536]{1,0:T(8,128)(2,1)}, u32[]{:S(2)}) copy-start(bf16[512,1536]{1,0:T(8,128)(2,1)} %weight_ref.5) | copy-start | bytes 4718596
  23.8 32.5 %copy-start.11 = (f32[2,512]{1,0:T(2,128)S(1)}, f32[2,512]{1,0:T(2,128)}, u32[]{:S(2)}) copy-start(f32[2,512]{1,0:T(2,128)} %gain_ref.11) | copy-start | bytes 12292
  23.9 32.5 %copy-start.12 = (f32[512]{0:T(512)S(1)}, f32[512]{0:T(512)}, u32[]{:S(2)}) copy-start(f32[512]{0:T(512)} %param.30) | copy-start | bytes 6148
  23.9 32.5 %copy-start.15 = (f32[64,512]{1,0:T(8,128)S(1)}, f32[64,512]{1,0:T(8,128)}, u32[]{:S(2)}) copy-start(f32[64,512]{1,0:T(8,128)} %constant.12.clone.sin_a) | copy-start | bytes 393220
  23.9 32.5 %copy-start.16 = (f32[64,512]{1,0:T(8,128)S(1)}, f32[64,512]{1,0:T(8,128)}, u32[]{:S(2)}) copy-start(f32[64,512]{1,0:T(8,128)} %constant.13.clone.cos_a) | copy-start | bytes 393220
  23.9 32.5 %copy-start.17 = (f32[32,512]{1,0:T(8,128)S(1)}, f32[32,512]{1,0:T(8,128)}, u32[]{:S(2)}) copy-start(f32[32,512]{1,0:T(8,128)} %constant.14.clone.sin_b) | copy-start | bytes 196612
  23.9 32.5 %copy-start.18 = (f32[32,512]{1,0:T(8,128)S(1)}, f32[32,512]{1,0:T(8,128)}, u32[]{:S(2)}) copy-start(f32[32,512]{1,0:T(8,128)} %constant.15.clone.cos_b) | copy-start | bytes 196612
  60.6 15.0 %collective-permute-start.4 = (bf16[1024,512]{1,0:T(8,128)(2,1)S(1)}, bf16[1024,512]{1,0:T(8,128)(2,1)S(1)}, u32[]{:S(2)}, u32[]{:S(2)}) collective-permute-start(bf16[1024,512]{1,0:T(8,128)(2,1)S(1)} %get-tuple-element.32.key_ref), channel_id=1, source_target_pairs={{0,1},{1,0},{2,3},{3,2},{4,5},{5,4},{6,7},{7,6},{8,9},{9,8},{10,11... | collective-permute-start | bytes 3145736 | tf_op jit(solution)/shard_map/ppermute | solution.py:479
  62.5 13.2 %collective-permute-start.5 = (bf16[512,1024]{1,0:T(8,128)(2,1)S(1)}, bf16[512,1024]{1,0:T(8,128)(2,1)S(1)}, u32[]{:S(2)}, u32[]{:S(2)}) collective-permute-start(bf16[512,1024]{1,0:T(8,128)(2,1)S(1)} %get-tuple-element.33.value_ref), channel_id=1, source_target_pairs={{0,1},{1,0},{2,3},{3,2},{4,5},{5,4},{6,7},{7,6},{8,9},{9,8},{10,11... | collective-permute-start | bytes 3145736 | tf_op jit(solution)/shard_map/ppermute | solution.py:479
  62.6 13.1 %copy-start.6 = (bf16[512,2048]{1,0:T(8,128)(2,1)S(1)}, bf16[512,2048]{1,0:T(8,128)(2,1)}, u32[]{:S(2)}) copy-start(bf16[512,2048]{1,0:T(8,128)(2,1)} %fc1_ref.1) | copy-start | bytes 6291460
  62.6 13.1 %copy-start.7 = (bf16[2048,512]{1,0:T(8,128)(2,1)S(1)}, bf16[2048,512]{1,0:T(8,128)(2,1)}, u32[]{:S(2)}) copy-start(bf16[2048,512]{1,0:T(8,128)(2,1)} %fc2_ref.1) | copy-start | bytes 6291460
  62.6 13.1 %copy-start.9 = (bf16[512,512]{1,0:T(8,128)(2,1)S(1)}, bf16[512,512]{1,0:T(8,128)(2,1)}, u32[]{:S(2)}) copy-start(bf16[512,512]{1,0:T(8,128)(2,1)} %out_weight_ref.1) | copy-start | bytes 1572868
  62.6 13.1 %copy-start.10 = (f32[2048]{0:T(1024)S(1)}, f32[2048]{0:T(1024)}, u32[]{:S(2)}) copy-start(f32[2048]{0:T(1024)} %param.37) | copy-start | bytes 24580
  62.6 13.1 %copy-start.13 = (f32[512]{0:T(512)S(1)}, f32[512]{0:T(512)}, u32[]{:S(2)}) copy-start(f32[512]{0:T(512)} %param.35) | copy-start | bytes 6148
  62.6 13.1 %copy-start.14 = (f32[512]{0:T(512)S(1)}, f32[512]{0:T(512)}, u32[]{:S(2)}) copy-start(f32[512]{0:T(512)} %param.39) | copy-start | bytes 6148
  (4 other events, 5.3 us)
